TPU v7x, 32 devices: a whole 2x2x4 slice. The times are simulated.
32 devices in a mesh: tm: 16 (over z, y, x), chan: 2 (over core).
Axes of the slice: x: 2, y: 2, z: 4, core: 2. Of those that a mesh axis runs over, the one named last changes fastest.
Arguments:
- strain: bfloat16 [128, 131072], P('chan', 'tm'), as said below
- fir_taps: float32 [128, 64], P('chan'), may hold values from -0.75 to 0.75
Outputs:
- factor: float32 [1024, 1024], P(('tm', 'chan'))
- whitened: bfloat16 [1024, 16384], P(None, ('tm', 'chan'))
Inputs may be any that keep to these rules, and one draw needn't show every extreme that they name: strain-rate samples of 128 channels.
All inputs are finite; a program needn't handle non-finite values.
Results may differ from a plain program's by a relative error of at most 0.001.
The roundings to bfloat16 on the way count: a program that leaves them out, or rounds other values in their place, can miss the bound.
Values may be sent and summed in bfloat16 or wider, within the bound.
A program may use at most 128 MiB of HBM per device.

v0:
```python
import jax
import jax.numpy as jnp
from jax import lax
from jax.sharding import PartitionSpec as P

LAGS = 8
TAPS = 64
STRIDE = 8


def shifted(value, axis, steps):
    count = lax.axis_size(axis)
    initial, last = (max(0, -steps), min(count, count - steps))
    return lax.ppermute(value, axis, [(source, source + steps) for source in range(initial, last)])


def decimate(extended, fir_taps, out_rows):
    channels = extended.shape[0]
    phases = jnp.transpose(extended.astype(jnp.float32).reshape(channels, -1, STRIDE), (0, 2, 1))
    running = jnp.zeros((channels, out_rows), jnp.float32)
    for j in range(TAPS // STRIDE):
        window = phases[:, :, j : j + out_rows]
        weights = fir_taps[:, j * STRIDE : (j + 1) * STRIDE]
        running = running + jnp.einsum(
            "csn,cs->cn", window, weights, precision=lax.Precision.HIGHEST
        )
    return running


def inner_gram(left_rows, right_rows):
    return lax.dot_general(
        left_rows, right_rows, (((1,), (1,)), ((), ())), preferred_element_type=jnp.float32
    )


def local(strain, fir_taps):
    samples = strain.shape[1]
    out_rows = samples // STRIDE
    rim_len = TAPS - STRIDE
    rim_raw = shifted(strain[:, :rim_len], "tm", -1)
    extended = jnp.concatenate([strain, rim_raw], axis=1)
    local_rows = decimate(extended, fir_taps, out_rows).astype(jnp.bfloat16)
    tail_rows = shifted(local_rows[:, : LAGS - 1], "tm", -1)
    decimated = jnp.concatenate([local_rows, tail_rows], axis=1)
    gathered = lax.all_gather(decimated, "chan", axis=0, tiled=True)
    row_count = out_rows // lax.axis_size("chan")
    first_col = lax.axis_index("chan") * row_count
    window = lax.dynamic_slice_in_dim(gathered, first_col, row_count + LAGS - 1, 1)
    hankel = jnp.concatenate([window[:, i : i + row_count] for i in range(LAGS)], axis=0)
    columns = hankel.shape[0]
    gram_full = lax.psum(inner_gram(hankel, hankel), ("tm", "chan"))
    devices_all = lax.axis_size(("tm", "chan"))
    covariance = gram_full / (row_count * devices_all)
    lower_factor = jnp.linalg.cholesky(covariance)
    factor_rows = columns // devices_all
    first_row = lax.axis_index(("tm", "chan")) * factor_rows
    factor_mine = lax.dynamic_slice_in_dim(lower_factor, first_row, factor_rows, 1).T
    whitened = jax.scipy.linalg.solve_triangular(
        lower_factor, hankel.astype(jnp.float32), lower=True
    )
    return (factor_mine, whitened.astype(jnp.bfloat16))


def solution(mesh):
    placed = (P("chan", "tm"), P("chan", None))
    return jax.shard_map(
        local,
        mesh=mesh,
        in_specs=placed,
        out_specs=(P(("tm", "chan"), None), P(None, ("tm", "chan"))),
        check_vma=False,
    )
```

profile of v0, /device:TPU:0, one launch (start us, length us, event | category | flops | bytes accessed | tf_op | source)
XLA Modules:
  0.0 586.8 jit_solution(7478276221011478313)
XLA Ops:
  10.4 4.1 collective-permute-done
  17.6 5.9 fusion.66
  23.5 4.4 copy.46
  27.9 4.3 copy.43
  32.1 4.3 copy.40
  36.4 3.3 copy.37
  39.8 4.4 copy.34
  44.2 4.3 copy.31
  48.5 4.3 copy.28
  52.8 2.7 copy.25
  55.5 2.3 fusion.75
  70.1 5.2 collective-permute-done.1
  78.4 3.3 fusion.76
  82.0 145.1 %all-reduce.3.cloned.1.call-done = f32[1024,1024]{0,1:T(8,128)} async-done(((f32[1024,1024]{0,1:T(8,128)}), f32[1024,1024]{0,1:T(8,128)}) %all-reduce.3.cloned.1.call-update) | async-done | bytes 4194320 | tf_op jit(solution)/shard_map/psum | solution.py:51
  227.0 5.0 broadcast_multiply_fusion
  232.0 5.5 copy.16
  237.6 4.4 fusion
  244.0 11.7 %cholesky.223 = f32[128,128]{1,0:T(8,128)S(1)} custom-call(f32[128,128]{1,0:T(8,128)S(1)} %cholesky.580), custom_call_target="Cholesky" | custom-call | tf_op jit(solution)/shard_map/jit(cholesky)/cholesky | solution.py:54
  255.7 9.8 %custom-call.63 = f32[1,128,128]{1,2,0:T(8,128)S(1)} custom-call(f32[1,128,128]{2,1,0:T(8,128)S(1)} %get-tuple-element.72), custom_call_target="InvertDiagBlocksLowerTriangular" | custom-call | tf_op jit(solution)/shard_map/jit(cholesky)/cholesky | solution.py:54
  267.2 2.7 convolution_subtract_fusion
  271.0 12.1 %cholesky.244 = f32[128,128]{1,0:T(8,128)S(1)} custom-call(f32[128,128]{1,0:T(8,128)S(1)} %cholesky.584), custom_call_target="Cholesky" | custom-call | tf_op jit(solution)/shard_map/jit(cholesky)/cholesky | solution.py:54
  283.1 2.5 cholesky.255
  287.1 9.8 %custom-call.64 = f32[1,128,128]{1,2,0:T(8,128)S(1)} custom-call(f32[1,128,128]{2,1,0:T(8,128)S(1)} %get-tuple-element.69), custom_call_target="InvertDiagBlocksLowerTriangular" | custom-call | tf_op jit(solution)/shard_map/jit(cholesky)/cholesky | solution.py:54
  300.3 11.7 %cholesky.468 = f32[128,128]{1,0:T(8,128)S(1)} custom-call(f32[128,128]{1,0:T(8,128)S(1)} %cholesky.589), custom_call_target="Cholesky" | custom-call | tf_op jit(solution)/shard_map/jit(cholesky)/cholesky | solution.py:54
  312.7 9.8 %custom-call.65 = f32[1,128,128]{1,2,0:T(8,128)S(1)} custom-call(f32[1,128,128]{2,1,0:T(8,128)S(1)} %get-tuple-element.66), custom_call_target="InvertDiagBlocksLowerTriangular" | custom-call | tf_op jit(solution)/shard_map/jit(cholesky)/cholesky | solution.py:54
  323.6 2.3 convolution_subtract_fusion.2
  326.0 11.9 %cholesky.487 = f32[128,128]{1,0:T(8,128)S(1)} custom-call(f32[128,128]{1,0:T(8,128)S(1)} %cholesky.594), custom_call_target="Cholesky" | custom-call | tf_op jit(solution)/shard_map/jit(cholesky)/cholesky | solution.py:54
  338.5 9.8 %custom-call.66 = f32[1,128,128]{1,2,0:T(8,128)S(1)} custom-call(f32[1,128,128]{2,1,0:T(8,128)S(1)} %get-tuple-element.63), custom_call_target="InvertDiagBlocksLowerTriangular" | custom-call | tf_op jit(solution)/shard_map/jit(cholesky)/cholesky | solution.py:54
  349.4 2.3 convolution_subtract_fusion.10
  351.8 11.7 %cholesky.506 = f32[128,128]{1,0:T(8,128)S(1)} custom-call(f32[128,128]{1,0:T(8,128)S(1)} %cholesky.599), custom_call_target="Cholesky" | custom-call | tf_op jit(solution)/shard_map/jit(cholesky)/cholesky | solution.py:54
  364.1 10.0 %custom-call.67 = f32[1,128,128]{1,2,0:T(8,128)S(1)} custom-call(f32[1,128,128]{2,1,0:T(8,128)S(1)} %get-tuple-element.60), custom_call_target="InvertDiagBlocksLowerTriangular" | custom-call | tf_op jit(solution)/shard_map/jit(cholesky)/cholesky | solution.py:54
  375.2 2.3 convolution_subtract_fusion.11
  377.5 11.7 %cholesky.526 = f32[128,128]{1,0:T(8,128)S(1)} custom-call(f32[128,128]{1,0:T(8,128)S(1)} %cholesky.604), custom_call_target="Cholesky" | custom-call | tf_op jit(solution)/shard_map/jit(cholesky)/cholesky | solution.py:54
  389.8 9.8 %custom-call.68 = f32[1,128,128]{1,2,0:T(8,128)S(1)} custom-call(f32[1,128,128]{2,1,0:T(8,128)S(1)} %get-tuple-element.57), custom_call_target="InvertDiagBlocksLowerTriangular" | custom-call | tf_op jit(solution)/shard_map/jit(cholesky)/cholesky | solution.py:54
  402.6 12.1 %cholesky.546 = f32[128,128]{1,0:T(8,128)S(1)} custom-call(f32[128,128]{1,0:T(8,128)S(1)} %cholesky.609), custom_call_target="Cholesky" | custom-call | tf_op jit(solution)/shard_map/jit(cholesky)/cholesky | solution.py:54
  415.3 9.8 %custom-call.69 = f32[1,128,128]{1,2,0:T(8,128)S(1)} custom-call(f32[1,128,128]{2,1,0:T(8,128)S(1)} %get-tuple-element.54), custom_call_target="InvertDiagBlocksLowerTriangular" | custom-call | tf_op jit(solution)/shard_map/jit(cholesky)/cholesky | solution.py:54
  427.8 11.7 %cholesky.564 = f32[128,128]{1,0:T(8,128)S(1)} custom-call(f32[128,128]{1,0:T(8,128)S(1)} %convolution_subtract_fusion.13), custom_call_target="Cholesky" | custom-call | tf_op jit(solution)/shard_map/jit(cholesky)/cholesky | solution.py:54
  449.7 4.8 fusion.1
  455.6 27.7 %while.1 = (s32[]{:T(128)}, f32[1024,1024]{1,0:T(8,128)}, s32[8,2]{0,1:T(2,128)S(1)}, f32[8,128,128]{2,1,0:T(8,128)}, s32[]{:T(128)}) while((s32[]{:T(128)}, f32[1024,1024]{1,0:T(8,128)}, s32[8,2]{0,1:T(2,128)S(1)}, f32[8,128,128]{2,1,0:T(8,128)}, s32[]{:T(128)}) %tuple.73), condition=%wide.while_cond, body=%wide.while_body.sunk | while | flops 2 | bytes 132205 | solution.py:58
  456.2 2.9 bitcast_dynamic-update-slice_fusion.2
  459.7 2.9 bitcast_dynamic-update-slice_fusion.2
  463.1 2.9 bitcast_dynamic-update-slice_fusion.2
  466.6 2.9 bitcast_dynamic-update-slice_fusion.2
  470.1 2.9 bitcast_dynamic-update-slice_fusion.2
  473.6 2.9 bitcast_dynamic-update-slice_fusion.2
  477.0 2.9 bitcast_dynamic-update-slice_fusion.2
  480.5 2.8 bitcast_dynamic-update-slice_fusion.2
  483.3 79.6 %custom-call.70 = f32[8,128,128]{1,2,0:T(8,128)S(1)} custom-call(f32[8,128,128]{2,1,0:T(8,128)} %get-tuple-element.9), custom_call_target="InvertDiagBlocksLowerTriangular" | custom-call | tf_op jit(solution)/shard_map/jit(_solve_triangular)/triangular_solve | solution.py:58
  (121 shorter events, 71.4 us)
Async XLA Ops:
  7.2 219.9 %all-reduce.3.cloned.1.call-start = ((), (), s32[]{:S(2)}) async-start(), calls=%async_computation | async-start | bytes 8388608 | tf_op jit(solution)/shard_map/psum | solution.py:51
  7.9 6.5 %collective-permute-start = (bf16[64,56]{1,0:T(8,128)(2,1)S(1)}, bf16[64,56]{1,0:T(8,128)(2,1)S(1)}, u32[]{:S(2)}, u32[]{:S(2)}) collective-permute-start(bf16[64,56]{1,0:T(8,128)(2,1)S(1)} %slice.324), channel_id=1, source_target_pairs={{2,0},{4,2},{6,4},{8,6},{10,8},{12,10},{14,12},{16,14},{18,16},{20... | collective-permute-start | bytes 21512 | tf_op jit(solution)/shard_map/ppermute | solution.py:14
  23.5 12.9 %copy-start.2 = (bf16[64,8,1024]{0,1,2:T(8,128)(2,1)S(1)}, bf16[64,8,1024]{0,1,2:T(8,128)(2,1)}, u32[]{:S(2)}) copy-start(bf16[64,8,1024]{0,1,2:T(8,128)(2,1)} %get-tuple-element.30) | copy-start | bytes 3145732
  39.8 13.0 %copy-start.1 = (bf16[64,8,1024]{0,1,2:T(8,128)(2,1)S(1)}, bf16[64,8,1024]{0,1,2:T(8,128)(2,1)}, u32[]{:S(2)}) copy-start(bf16[64,8,1024]{0,1,2:T(8,128)(2,1)} %get-tuple-element.26) | copy-start | bytes 3145732
  55.5 9.0 %copy-start.5 = (bf16[64,8,1024]{2,1,0:T(8,128)(2,1)S(1)}, bf16[64,8,1024]{2,1,0:T(8,128)(2,1)}, u32[]{:S(2)}) copy-start(bf16[64,8,1024]{2,1,0:T(8,128)(2,1)} %copy.34) | copy-start | bytes 3145732
  55.5 10.0 %copy-start.4 = (bf16[64,8,1024]{2,1,0:T(8,128)(2,1)S(1)}, bf16[64,8,1024]{2,1,0:T(8,128)(2,1)}, u32[]{:S(2)}) copy-start(bf16[64,8,1024]{2,1,0:T(8,128)(2,1)} %copy.31) | copy-start | bytes 3145732
  55.5 10.9 %copy-start.3 = (bf16[64,8,1024]{2,1,0:T(8,128)(2,1)S(1)}, bf16[64,8,1024]{2,1,0:T(8,128)(2,1)}, u32[]{:S(2)}) copy-start(bf16[64,8,1024]{2,1,0:T(8,128)(2,1)} %copy.28) | copy-start | bytes 3145732
  68.8 6.5 %collective-permute-start.1 = (bf16[64,7]{1,0:T(8,128)(2,1)S(1)}, bf16[64,7]{1,0:T(8,128)(2,1)S(1)}, u32[]{:S(2)}, u32[]{:S(2)}) collective-permute-start(bf16[64,7]{1,0:T(8,128)(2,1)S(1)} %slice.369), channel_id=1, source_target_pairs={{2,0},{4,2},{6,4},{8,6},{10,8},{12,10},{14,12},{16,14},{18,16},{20... | collective-permute-start | bytes 2696 | tf_op jit(solution)/shard_map/ppermute | solution.py:14
  242.0 1.9 copy-start
  270.1 26.8 %copy-start.6 = (f32[896,128]{1,0:T(8,128)S(1)}, f32[896,128]{1,0:T(8,128)}, u32[]{:S(2)}) copy-start(f32[896,128]{1,0:T(8,128)} %convolution_subtract_fusion) | copy-start | bytes 1376260
  578.7 1.0 copy-start.7
Sparse Core Ops, SparseCore 0:
  81.8 145.2 all-reduce.2
where the time goes:
time: 596 us; the launch traced here: 587 us
  other arithmetic  268 us (45%)
  waiting for transfers between devices  154 us (26%)
  local copies, waits for them, and re-layouts  84.7 us (14%)
  matrix products  54.8 us (9%)
  between operations  19.8 us (3%)
    another operation x30, other arithmetic, local(): lower_factor = jnp.linalg.cholesky(covariance)  173 us
    psum x1, waiting for transfers between devices, local(): gram_full = lax.psum(inner_gram(hankel, hankel), ('tm', 'chan'))  145 us
    another operation x3, other arithmetic, local(): jax.scipy.linalg.solve_triangular(lower_factor, hankel.astype(jnp.float32...  84.4 us
    slice x9, local copies, waits for them, and re-layouts, decimate(): window = phases[:, :, j:j + out_rows]  37.8 us
    another operation x24, local copies, waits for them, and re-layouts  27.7 us
    another operation x14, matrix products, local(): lower_factor = jnp.linalg.cholesky(covariance)  23.5 us
    another operation x15, matrix products, local(): jax.scipy.linalg.solve_triangular(lower_factor, hankel.astype(jnp.float32...  15.2 us
    dot_general x8, matrix products, decimate(): jnp.einsum('csn,cs->cn', window, weights, precision=lax.Precision.HIGHEST)  12.8 us
  transfers between devices with their start and end apart: 3, of which 3 were waited for; matrix products, arithmetic and copies ran while one was open for 0% of the time, Pallas kernels for 0%

commit v1 on v0

--- a/solution.py
+++ b/solution.py
@@ -48,7 +48,7 @@
     window = lax.dynamic_slice_in_dim(gathered, first_col, row_count + LAGS - 1, 1)
     hankel = jnp.concatenate([window[:, i : i + row_count] for i in range(LAGS)], axis=0)
     columns = hankel.shape[0]
-    gram_full = lax.psum(inner_gram(hankel, hankel), ("tm", "chan"))
+    gram_full = lax.psum(lax.psum(inner_gram(hankel, hankel), "chan"), "tm")
     devices_all = lax.axis_size(("tm", "chan"))
     covariance = gram_full / (row_count * devices_all)
     lower_factor = jnp.linalg.cholesky(covariance)

time: 596 us -> 658 us (1.10)
  waiting for transfers between devices: 154 us -> 217 us
    psum x1 -> x2, waiting for transfers between devices: 145 us -> 208 us  [local(): gram_full = lax.psum(lax.psum(inner_gram(hankel, hankel), 'chan'), 'tm')]
  transfers between devices with their start and end apart: 3 -> 4, of which waited for: 3 -> 4; matrix products, arithmetic and copies ran while one was open for 0% -> 0% of each run, Pallas kernels for 0% -> 0%
where the time goes in v1:
time: 658 us; the launch traced here: 649 us
  other arithmetic  268 us (41%)
  waiting for transfers between devices  217 us (33%)
  local copies, waits for them, and re-layouts  84.7 us (13%)
  matrix products  54.8 us (8%)
  between operations  19.8 us (3%)
    psum x2, waiting for transfers between devices, local(): gram_full = lax.psum(lax.psum(inner_gram(hankel, hankel), 'chan'), 'tm')  208 us
    another operation x30, other arithmetic, local(): lower_factor = jnp.linalg.cholesky(covariance)  173 us
    another operation x3, other arithmetic, local(): jax.scipy.linalg.solve_triangular(lower_factor, hankel.astype(jnp.float32...  84.4 us
    slice x9, local copies, waits for them, and re-layouts, decimate(): window = phases[:, :, j:j + out_rows]  37.8 us
    another operation x24, local copies, waits for them, and re-layouts  27.7 us
    another operation x14, matrix products, local(): lower_factor = jnp.linalg.cholesky(covariance)  23.5 us
    another operation x15, matrix products, local(): jax.scipy.linalg.solve_triangular(lower_factor, hankel.astype(jnp.float32...  15.2 us
  transfers between devices with their start and end apart: 4, of which 4 were waited for; matrix products, arithmetic and copies ran while one was open for 0% of the time, Pallas kernels for 0%

profile of v1, /device:TPU:0, one launch (start us, length us, event | category | flops | bytes accessed | tf_op | source)
XLA Modules:
  0.0 649.3 jit_solution(8270675653038545018)
XLA Ops:
  10.4 4.1 collective-permute-done
  17.6 5.9 fusion.66
  23.5 4.4 copy.46
  27.9 4.3 copy.43
  32.1 4.3 copy.40
  36.4 3.3 copy.37
  39.8 4.4 copy.34
  44.2 4.3 copy.31
  48.5 4.3 copy.28
  52.8 2.7 copy.25
  55.5 2.3 fusion.75
  70.1 5.2 collective-permute-done.1
  78.4 3.2 fusion.76
  81.6 32.0 %all-reduce.4.cloned.1.call-done = f32[1024,1024]{0,1:T(8,128)} async-done(((f32[1024,1024]{0,1:T(8,128)}), f32[1024,1024]{0,1:T(8,128)}) %all-reduce.4.cloned.1.call-update) | async-done | bytes 4194320 | tf_op jit(solution)/shard_map/psum | solution.py:51
  114.0 175.6 %all-reduce.6.cloned.1.call-done = f32[1024,1024]{0,1:T(8,128)} async-done(((f32[1024,1024]{0,1:T(8,128)}), f32[1024,1024]{0,1:T(8,128)}) %all-reduce.6.cloned.1.call-update) | async-done | bytes 4194320 | tf_op jit(solution)/shard_map/psum | solution.py:51
  289.5 5.0 broadcast_multiply_fusion
  294.5 5.5 copy.16
  300.1 4.4 fusion
  306.5 11.7 %cholesky.223 = f32[128,128]{1,0:T(8,128)S(1)} custom-call(f32[128,128]{1,0:T(8,128)S(1)} %cholesky.580), custom_call_target="Cholesky" | custom-call | tf_op jit(solution)/shard_map/jit(cholesky)/cholesky | solution.py:54
  318.2 9.8 %custom-call.63 = f32[1,128,128]{1,2,0:T(8,128)S(1)} custom-call(f32[1,128,128]{2,1,0:T(8,128)S(1)} %get-tuple-element.72), custom_call_target="InvertDiagBlocksLowerTriangular" | custom-call | tf_op jit(solution)/shard_map/jit(cholesky)/cholesky | solution.py:54
  329.7 2.7 convolution_subtract_fusion
  333.6 12.1 %cholesky.244 = f32[128,128]{1,0:T(8,128)S(1)} custom-call(f32[128,128]{1,0:T(8,128)S(1)} %cholesky.584), custom_call_target="Cholesky" | custom-call | tf_op jit(solution)/shard_map/jit(cholesky)/cholesky | solution.py:54
  345.6 2.5 cholesky.255
  349.7 9.8 %custom-call.64 = f32[1,128,128]{1,2,0:T(8,128)S(1)} custom-call(f32[1,128,128]{2,1,0:T(8,128)S(1)} %get-tuple-element.69), custom_call_target="InvertDiagBlocksLowerTriangular" | custom-call | tf_op jit(solution)/shard_map/jit(cholesky)/cholesky | solution.py:54
  362.8 11.7 %cholesky.468 = f32[128,128]{1,0:T(8,128)S(1)} custom-call(f32[128,128]{1,0:T(8,128)S(1)} %cholesky.589), custom_call_target="Cholesky" | custom-call | tf_op jit(solution)/shard_map/jit(cholesky)/cholesky | solution.py:54
  375.2 9.8 %custom-call.65 = f32[1,128,128]{1,2,0:T(8,128)S(1)} custom-call(f32[1,128,128]{2,1,0:T(8,128)S(1)} %get-tuple-element.66), custom_call_target="InvertDiagBlocksLowerTriangular" | custom-call | tf_op jit(solution)/shard_map/jit(cholesky)/cholesky | solution.py:54
  386.2 2.3 convolution_subtract_fusion.2
  388.5 11.9 %cholesky.487 = f32[128,128]{1,0:T(8,128)S(1)} custom-call(f32[128,128]{1,0:T(8,128)S(1)} %cholesky.594), custom_call_target="Cholesky" | custom-call | tf_op jit(solution)/shard_map/jit(cholesky)/cholesky | solution.py:54
  401.0 9.8 %custom-call.66 = f32[1,128,128]{1,2,0:T(8,128)S(1)} custom-call(f32[1,128,128]{2,1,0:T(8,128)S(1)} %get-tuple-element.63), custom_call_target="InvertDiagBlocksLowerTriangular" | custom-call | tf_op jit(solution)/shard_map/jit(cholesky)/cholesky | solution.py:54
  411.9 2.3 convolution_subtract_fusion.10
  414.3 11.7 %cholesky.506 = f32[128,128]{1,0:T(8,128)S(1)} custom-call(f32[128,128]{1,0:T(8,128)S(1)} %cholesky.599), custom_call_target="Cholesky" | custom-call | tf_op jit(solution)/shard_map/jit(cholesky)/cholesky | solution.py:54
  426.6 10.0 %custom-call.67 = f32[1,128,128]{1,2,0:T(8,128)S(1)} custom-call(f32[1,128,128]{2,1,0:T(8,128)S(1)} %get-tuple-element.60), custom_call_target="InvertDiagBlocksLowerTriangular" | custom-call | tf_op jit(solution)/shard_map/jit(cholesky)/cholesky | solution.py:54
  440.0 11.7 %cholesky.526 = f32[128,128]{1,0:T(8,128)S(1)} custom-call(f32[128,128]{1,0:T(8,128)S(1)} %cholesky.604), custom_call_target="Cholesky" | custom-call | tf_op jit(solution)/shard_map/jit(cholesky)/cholesky | solution.py:54
  452.3 9.8 %custom-call.68 = f32[1,128,128]{1,2,0:T(8,128)S(1)} custom-call(f32[1,128,128]{2,1,0:T(8,128)S(1)} %get-tuple-element.57), custom_call_target="InvertDiagBlocksLowerTriangular" | custom-call | tf_op jit(solution)/shard_map/jit(cholesky)/cholesky | solution.py:54
  465.1 12.1 %cholesky.546 = f32[128,128]{1,0:T(8,128)S(1)} custom-call(f32[128,128]{1,0:T(8,128)S(1)} %cholesky.609), custom_call_target="Cholesky" | custom-call | tf_op jit(solution)/shard_map/jit(cholesky)/cholesky | solution.py:54
  477.9 9.8 %custom-call.69 = f32[1,128,128]{1,2,0:T(8,128)S(1)} custom-call(f32[1,128,128]{2,1,0:T(8,128)S(1)} %get-tuple-element.54), custom_call_target="InvertDiagBlocksLowerTriangular" | custom-call | tf_op jit(solution)/shard_map/jit(cholesky)/cholesky | solution.py:54
  490.3 11.7 %cholesky.564 = f32[128,128]{1,0:T(8,128)S(1)} custom-call(f32[128,128]{1,0:T(8,128)S(1)} %convolution_subtract_fusion.13), custom_call_target="Cholesky" | custom-call | tf_op jit(solution)/shard_map/jit(cholesky)/cholesky | solution.py:54
  512.2 4.8 fusion.1
  518.1 27.7 %while.1 = (s32[]{:T(128)}, f32[1024,1024]{1,0:T(8,128)}, s32[8,2]{0,1:T(2,128)S(1)}, f32[8,128,128]{2,1,0:T(8,128)}, s32[]{:T(128)}) while((s32[]{:T(128)}, f32[1024,1024]{1,0:T(8,128)}, s32[8,2]{0,1:T(2,128)S(1)}, f32[8,128,128]{2,1,0:T(8,128)}, s32[]{:T(128)}) %tuple.73), condition=%wide.while_cond, body=%wide.while_body.sunk | while | flops 2 | bytes 132205 | solution.py:58
  518.7 2.9 bitcast_dynamic-update-slice_fusion.2
  522.2 2.9 bitcast_dynamic-update-slice_fusion.2
  525.6 2.9 bitcast_dynamic-update-slice_fusion.2
  529.1 2.9 bitcast_dynamic-update-slice_fusion.2
  532.6 2.9 bitcast_dynamic-update-slice_fusion.2
  536.1 2.9 bitcast_dynamic-update-slice_fusion.2
  539.5 2.9 bitcast_dynamic-update-slice_fusion.2
  543.0 2.8 bitcast_dynamic-update-slice_fusion.2
  545.8 79.6 %custom-call.70 = f32[8,128,128]{1,2,0:T(8,128)S(1)} custom-call(f32[8,128,128]{2,1,0:T(8,128)} %get-tuple-element.9), custom_call_target="InvertDiagBlocksLowerTriangular" | custom-call | tf_op jit(solution)/shard_map/jit(_solve_triangular)/triangular_solve | solution.py:58
  (124 shorter events, 73.7 us)
Async XLA Ops:
  7.2 106.5 %all-reduce.4.cloned.1.call-start = ((), (), s32[]{:S(2)}) async-start(), calls=%async_computation | async-start | bytes 8388608 | tf_op jit(solution)/shard_map/psum | solution.py:51
  7.9 6.5 %collective-permute-start = (bf16[64,56]{1,0:T(8,128)(2,1)S(1)}, bf16[64,56]{1,0:T(8,128)(2,1)S(1)}, u32[]{:S(2)}, u32[]{:S(2)}) collective-permute-start(bf16[64,56]{1,0:T(8,128)(2,1)S(1)} %slice.324), channel_id=1, source_target_pairs={{2,0},{4,2},{6,4},{8,6},{10,8},{12,10},{14,12},{16,14},{18,16},{20... | collective-permute-start | bytes 21512 | tf_op jit(solution)/shard_map/ppermute | solution.py:14
  23.5 12.9 %copy-start.2 = (bf16[64,8,1024]{0,1,2:T(8,128)(2,1)S(1)}, bf16[64,8,1024]{0,1,2:T(8,128)(2,1)}, u32[]{:S(2)}) copy-start(bf16[64,8,1024]{0,1,2:T(8,128)(2,1)} %get-tuple-element.30) | copy-start | bytes 3145732
  39.8 13.0 %copy-start.1 = (bf16[64,8,1024]{0,1,2:T(8,128)(2,1)S(1)}, bf16[64,8,1024]{0,1,2:T(8,128)(2,1)}, u32[]{:S(2)}) copy-start(bf16[64,8,1024]{0,1,2:T(8,128)(2,1)} %get-tuple-element.26) | copy-start | bytes 3145732
  55.5 9.0 %copy-start.5 = (bf16[64,8,1024]{2,1,0:T(8,128)(2,1)S(1)}, bf16[64,8,1024]{2,1,0:T(8,128)(2,1)}, u32[]{:S(2)}) copy-start(bf16[64,8,1024]{2,1,0:T(8,128)(2,1)} %copy.34) | copy-start | bytes 3145732
  55.5 10.0 %copy-start.4 = (bf16[64,8,1024]{2,1,0:T(8,128)(2,1)S(1)}, bf16[64,8,1024]{2,1,0:T(8,128)(2,1)}, u32[]{:S(2)}) copy-start(bf16[64,8,1024]{2,1,0:T(8,128)(2,1)} %copy.31) | copy-start | bytes 3145732
  55.5 10.9 %copy-start.3 = (bf16[64,8,1024]{2,1,0:T(8,128)(2,1)S(1)}, bf16[64,8,1024]{2,1,0:T(8,128)(2,1)}, u32[]{:S(2)}) copy-start(bf16[64,8,1024]{2,1,0:T(8,128)(2,1)} %copy.28) | copy-start | bytes 3145732
  68.8 6.5 %collective-permute-start.1 = (bf16[64,7]{1,0:T(8,128)(2,1)S(1)}, bf16[64,7]{1,0:T(8,128)(2,1)S(1)}, u32[]{:S(2)}, u32[]{:S(2)}) collective-permute-start(bf16[64,7]{1,0:T(8,128)(2,1)S(1)} %slice.369), channel_id=1, source_target_pairs={{2,0},{4,2},{6,4},{8,6},{10,8},{12,10},{14,12},{16,14},{18,16},{20... | collective-permute-start | bytes 2696 | tf_op jit(solution)/shard_map/ppermute | solution.py:14
  81.6 207.9 %all-reduce.6.cloned.1.call-start = ((), (), s32[]{:S(2)}) async-start(), calls=%async_computation.1 | async-start | bytes 8388608 | tf_op jit(solution)/shard_map/psum | solution.py:51
  304.5 1.9 copy-start
  332.6 26.8 %copy-start.6 = (f32[896,128]{1,0:T(8,128)S(1)}, f32[896,128]{1,0:T(8,128)}, u32[]{:S(2)}) copy-start(f32[896,128]{1,0:T(8,128)} %convolution_subtract_fusion) | copy-start | bytes 1376260
  641.3 1.0 copy-start.7
Sparse Core Ops, SparseCore 0:
  81.7 31.8 all-reduce.3
  120.2 169.2 all-reduce.5
